TPU v7x, 32 devices: a whole 2x2x4 slice. The times are simulated.
32 devices in a mesh: grp: 2 (over x), ch: 16 (over z, y, core).
Axes of the slice: x: 2, y: 2, z: 4, core: 2. Of those that a mesh axis runs over, the one named last changes fastest.
Arguments:
- features: bfloat16 [2048, 2048], P('ch', 'grp'), parts along dimension 1, may hold values from -50 to 50
- dw_weight: float32 [2048, 49], P('ch'), may hold values from -0.875 to 0.875
- norm_gain: float32 [2048], replicated, may hold values from 0.25 to 1.75
- layer_scale: float32 [2048], replicated, may hold values from 0.2 to 1
- w_in: bfloat16 [8192, 2048], P('ch'), may hold values from -0.125 to 0.125
- w_out: bfloat16 [8192, 2048], P('ch'), may hold values from -0.0625 to 0.0625
- w_head: bfloat16 [2048, 150], replicated, may hold values from -3 to 3
- labels: int32 [2048], P('grp'), parts along dimension 0, may hold values from 0 to 149
Outputs:
- d_features: float32 [2048, 2048], P('ch', 'grp'), parts along dimension 1
- d_dw: float32 [2048, 98], P('ch', 'grp'), parts along dimension 1
- d_scale: float32 [4096], P(('grp', 'ch')), parts along dimension 0
- d_w_in: float32 [16384, 2048], P(('grp', 'ch')), parts along dimension 0
- d_w_out: float32 [16384, 2048], P(('grp', 'ch')), parts along dimension 0
- d_head: float32 [2048, 300], P('ch', 'grp'), parts along dimension 1
- mean_loss: float32 [2], P('grp'), parts along dimension 0
There are 2 independent parts, one for each index of `grp`. A program takes and returns all parts, laid end to end along the dimension named above; an argument that names none is the same for every part. Nothing has to cross between parts.
All inputs are finite; a program needn't handle non-finite values.
Results may differ from a plain program's by a relative error of at most 0.012.
Values may be sent and summed in bfloat16 or wider, within the bound.
A program may use at most 128 MiB of HBM per device.

v0:
```python
import jax
import jax.numpy as jnp
from jax import lax
from jax.sharding import PartitionSpec as P

KS = 7
WIN_H = 32
WIN_W = 32
norm_eps = 1e-06


def conv_apply(in_grid, kernel):
    half = KS // 2
    padded = jnp.pad(in_grid, ((0, 0), (half, half), (half, half)))
    running = jnp.zeros(in_grid.shape, in_grid.dtype)
    for row_shift in range(KS):
        for col_shift in range(KS):
            tap = kernel[:, row_shift * KS + col_shift]
            running = (
                running
                + tap[:, None, None]
                * padded[:, row_shift : row_shift + WIN_H, col_shift : col_shift + WIN_W]
            )
    return running


def gelu_parts(values):
    cum_prob = 0.5 * (1.0 + lax.erf(values * 0.7071067811865476))
    density = jnp.exp(-0.5 * values * values) * 0.3989422804014327
    return (values * cum_prob, cum_prob + values * density)


def per_device(features, dw_weight, norm_gain, layer_scale, w_in, w_out, w_head, labels):
    highest = lax.Precision.HIGHEST
    my_rows = features.shape[0]
    tok_count = features.shape[1]
    class_count = w_head.shape[1]
    row_offset = lax.axis_index("ch") * my_rows
    inputs_wide = features.astype(jnp.float32)
    in_grid = inputs_wide.reshape(my_rows, WIN_H, WIN_W)
    conv_out = conv_apply(in_grid, dw_weight).reshape(my_rows, tok_count).astype(jnp.bfloat16)
    conv_all = lax.all_gather(conv_out, "ch", axis=0, tiled=True)
    conv_wide = conv_all.astype(jnp.float32)
    tok_mean = jnp.mean(conv_wide, axis=0)
    centered = conv_wide - tok_mean[None, :]
    tok_var = jnp.mean(centered * centered, axis=0)
    inv_std = 1.0 / jnp.sqrt(tok_var + norm_eps)
    normed = centered * inv_std[None, :]
    norm_out = (norm_gain[:, None] * normed).astype(jnp.bfloat16)
    pre_act = jnp.dot(w_in, norm_out, preferred_element_type=jnp.float32)
    gelu_out, gelu_slope = gelu_parts(pre_act)
    hidden = gelu_out.astype(jnp.bfloat16)
    my_scale = lax.dynamic_slice_in_dim(layer_scale, row_offset, my_rows, 0)
    head_wide = w_head.astype(jnp.float32)
    my_head = lax.dynamic_slice_in_dim(head_wide, row_offset, my_rows, 0)
    w_cols = w_out
    branch_sum = lax.psum_scatter(
        lax.dot_general(
            w_cols, hidden, (((0,), (0,)), ((), ())), preferred_element_type=jnp.float32
        ),
        "ch",
        scatter_dimension=0,
        tiled=True,
    )
    block_out = inputs_wide + my_scale[:, None] * branch_sum
    part_logits = lax.dot_general(block_out, my_head, (((0,), (0,)), ((), ())), precision=highest)
    logits = lax.psum(part_logits, "ch")
    row_max = jnp.max(logits, axis=1, keepdims=True)
    exp_terms = jnp.exp(logits - row_max)
    exp_total = jnp.sum(exp_terms, axis=1, keepdims=True)
    log_total = jnp.log(exp_total) + row_max
    onehot = (labels[:, None] == jnp.arange(class_count, dtype=jnp.int32)[None, :]).astype(
        jnp.float32
    )
    picked = jnp.sum(logits * onehot, axis=1)
    mean_loss = jnp.mean(log_total[:, 0] - picked).reshape(1)
    logit_grad = exp_terms / exp_total - onehot
    out_grad = lax.dot_general(my_head, logit_grad, (((1,), (1,)), ((), ())), precision=highest)
    d_head = jnp.dot(block_out, logit_grad, precision=highest)
    d_scale = jnp.sum(out_grad * branch_sum, axis=1)
    branch_grad = (my_scale[:, None] * out_grad).astype(jnp.bfloat16)
    incoming = lax.all_gather(branch_grad, "ch", axis=0, tiled=True)
    w_cols = w_out
    hidden_acc = jnp.dot(w_cols, incoming, preferred_element_type=jnp.float32)
    tile_grad = lax.dot_general(
        hidden, incoming, (((1,), (1,)), ((), ())), preferred_element_type=jnp.float32
    )
    pre_grad = (hidden_acc * gelu_slope).astype(jnp.bfloat16)
    d_w_in = lax.dot_general(
        pre_grad, norm_out, (((1,), (1,)), ((), ())), preferred_element_type=jnp.float32
    )
    norm_grad = lax.dot_general(
        w_in, pre_grad, (((0,), (0,)), ((), ())), preferred_element_type=jnp.float32
    )
    gained = norm_gain[:, None] * norm_grad
    conv_term = (
        gained
        - jnp.mean(gained, axis=0)[None, :]
        - normed * jnp.mean(gained * normed, axis=0)[None, :]
    ) * inv_std[None, :]
    conv_grad = lax.psum_scatter(conv_term, "ch", scatter_dimension=0, tiled=True)
    unused, pullback = jax.vjp(conv_apply, in_grid, dw_weight)
    grid_grad, d_dw = pullback(conv_grad.reshape(my_rows, WIN_H, WIN_W))
    d_features = out_grad + grid_grad.reshape(my_rows, tok_count)
    return (d_features, d_dw, d_scale, d_w_in, tile_grad, d_head, mean_loss)


def solution(mesh):
    placed = (P("ch", "grp"), P("ch", None), P(), P(), P("ch", None), P("ch", None), P(), P("grp"))
    return jax.shard_map(
        per_device,
        mesh=mesh,
        in_specs=placed,
        out_specs=(
            P("ch", "grp"),
            P("ch", "grp"),
            P(("grp", "ch")),
            P(("grp", "ch"), None),
            P(("grp", "ch"), None),
            P("ch", "grp"),
            P("grp"),
        ),
        check_vma=False,
    )
```

profile of v0, /device:TPU:0, one launch (start us, length us, event | category | flops | bytes accessed | tf_op | source)
XLA Modules:
  0.0 497.7 jit_solution(14007070145774544614)
XLA Ops:
  11.6 4.8 add_convert_fusion
  16.5 56.0 %all-gather.3.cloned.1.call-done = bf16[2048,1024]{0,1:T(8,128)(2,1)} async-done(((bf16[128,1024]{0,1:T(8,128)(2,1)}), bf16[2048,1024]{0,1:T(8,128)(2,1)}) %all-gather.3.cloned.1.call-update) | async-done | bytes 4194320 | tf_op jit(solution)/shard_map/all_gather | solution.py:42
  72.5 3.0 convert_reduce_fusion
  77.3 1.6 fusion.5
  79.0 2.4 fusion.31
  82.7 5.6 %convolution_bitcast_fusion = f32[2048,1024]{0,1:T(8,128)} fusion(bf16[512,2048]{1,0:T(8,128)(2,1)S(1)} %copy-done.45, f32[1024,512]{1,0:T(8,128)S(1)} %fusion.31), kind=kOutput, calls=%fused_computation.62 | convolution fusion | flops 2150105088 | bytes 12582912 | tf_op jit(solution)/shard_map/dot_general | solution.py:58
  89.2 102.4 %reduce-scatter.3.cloned.1.call-done = f32[128,1024]{0,1:T(8,128)} async-done(((f32[2048,1024]{0,1:T(8,128)}), f32[128,1024]{0,1:T(8,128)}) %reduce-scatter.3.cloned.1.call-update) | async-done | bytes 524304 | tf_op jit(solution)/shard_map/reduce_scatter | solution.py:57
  191.5 2.6 fusion.22
  194.2 91.7 %all-reduce.101.cloned.1.call-done = f32[1024,150]{0,1:T(8,128)} async-done(((f32[1024,150]{0,1:T(8,128)}), f32[1024,150]{0,1:T(8,128)}) %all-reduce.101.cloned.1.call-update) | async-done | bytes 614416 | tf_op jit(solution)/shard_map/psum | solution.py:67
  288.2 1.7 fusion.23
  290.9 2.5 multiply_reduce_fusion.1
  293.7 53.5 %all-gather.5.cloned.1.call-done = bf16[2048,1024]{0,1:T(8,128)(2,1)} async-done(((bf16[128,1024]{0,1:T(8,128)(2,1)}), bf16[2048,1024]{0,1:T(8,128)(2,1)}) %all-gather.5.cloned.1.call-update) | async-done | bytes 4194320 | tf_op jit(solution)/shard_map/all_gather | solution.py:82
  347.2 6.5 %fusion.15 = bf16[512,1024]{0,1:T(8,128)(2,1)S(1)} fusion(f32[1024,512]{1,0:T(8,128)} %copy-done.7, bf16[2048,1024]{0,1:T(8,128)(2,1)} %all-gather.5.cloned.1.call-done, bf16[512,2048]{1,0:T(8,128)(2,1)} %param.13), kind=kOutput, calls=%fused_computation.69 | convolution fusion | flops 2152726528 | bytes 9437184 | tf_op jit(solution)/shard_map/dot_general | solution.py:84
  353.7 3.0 fusion.6
  357.3 5.4 %fusion.8 = f32[2048,1024]{0,1:T(8,128)} fusion(bf16[2048,1024]{0,1:T(8,128)(2,1)S(1)} %copy-done.3, f32[1024,2048]{1,0:T(8,128)S(1)} %get-tuple-element.158, f32[1024]{0:T(1024)S(1)} %get-tuple-element.159, f32[1024]{0:T(1024)S(1)} %get-tuple-element.160, f32[2048]{0:T(1024)S(1)} %copy-done.13, f32[1024]{0:T(1024)S(1)} %add_rsqrt_fusion, ...), kind=kLoop, calls=%fused_computation.10 | loop fusion | flops 16777216 | bytes 20996096 | tf_op jit(solution)/shard_map/mul | solution.py:96
  365.6 7.4 %fusion.32 = f32[512,2048]{1,0:T(8,128)} fusion(bf16[512,1024]{0,1:T(8,128)(2,1)} %copy-done.10, bf16[2048,1024]{0,1:T(8,128)(2,1)} %copy-done.4), kind=kOutput, calls=%fused_computation.255 | convolution fusion | flops 2147483648 | bytes 9437184 | tf_op jit(solution)/shard_map/dot_general | solution.py:89
  372.9 4.5 fusion.28
  377.5 88.5 %reduce-scatter.5.cloned.1.call-done = f32[128,1024]{0,1:T(8,128)} async-done(((f32[2048,1024]{0,1:T(8,128)}), f32[128,1024]{0,1:T(8,128)}) %reduce-scatter.5.cloned.1.call-update) | async-done | bytes 524304 | tf_op jit(solution)/shard_map/reduce_scatter | solution.py:101
  465.9 2.9 broadcast_multiply_fusion.2
  470.0 2.4 broadcast_multiply_fusion
  472.4 6.0 %pad_add_fusion = f32[128,38,38]{0,2,1:T(8,128)S(1)} fusion(f32[128,32,32]{0,2,1:T(8,128)S(1)} %get-tuple-element.66, f32[128,32,32]{0,2,1:T(8,128)S(1)} %get-tuple-element.67, f32[128,32,32]{0,2,1:T(8,128)S(1)} %get-tuple-element.68, f32[128,32,32]{0,2,1:T(8,128)S(1)} %get-tuple-element.69, f32[128,32,32]{0,2,1:T(8,128)S(1)} %get-tuple-element.70, ...), kind=kLoop, calls=%fused_computation.76 | loop fusion | flops 7762944 | bytes 23283712 | tf_op jit(solution)/shard_map/transpose(jvp())/add_any | solution.py:22
  478.4 3.1 pad_add_fusion.1
  481.5 2.1 copy.21
  483.5 2.1 add.438
  (124 shorter events, 20.1 us)
Async XLA Ops:
  7.2 71.8 %copy-start = (bf16[512,2048]{1,0:T(8,128)(2,1)S(1)}, bf16[512,2048]{1,0:T(8,128)(2,1)}, u32[]{:S(2)}) copy-start(bf16[512,2048]{1,0:T(8,128)(2,1)} %param.12) | copy-start | bytes 6291460
  7.2 65.3 %all-gather.3.cloned.1.call-start = ((), (), s32[]{:S(2)}) async-start(), calls=%async_computation.2 | async-start | bytes 4456448 | tf_op jit(solution)/shard_map/all_gather | solution.py:42
  9.2 67.9 %copy-start.29 = (f32[128]{0:T(128)}, f32[128]{0:T(128)S(1)}, u32[]{:S(2)}) copy-start(f32[128]{0:T(128)S(1)} %get-tuple-element.110) | copy-start | bytes 1540
  9.2 67.9 %copy-start.30 = (f32[128]{0:T(128)}, f32[128]{0:T(128)S(1)}, u32[]{:S(2)}) copy-start(f32[128]{0:T(128)S(1)} %get-tuple-element.111) | copy-start | bytes 1540
  9.2 67.9 %copy-start.31 = (f32[128]{0:T(128)}, f32[128]{0:T(128)S(1)}, u32[]{:S(2)}) copy-start(f32[128]{0:T(128)S(1)} %get-tuple-element.112) | copy-start | bytes 1540
  9.2 67.9 %copy-start.32 = (f32[128]{0:T(128)}, f32[128]{0:T(128)S(1)}, u32[]{:S(2)}) copy-start(f32[128]{0:T(128)S(1)} %get-tuple-element.113) | copy-start | bytes 1540
  9.3 67.9 %copy-start.33 = (f32[128]{0:T(128)}, f32[128]{0:T(128)S(1)}, u32[]{:S(2)}) copy-start(f32[128]{0:T(128)S(1)} %get-tuple-element.114) | copy-start | bytes 1540
  9.3 67.9 %copy-start.34 = (f32[128]{0:T(128)}, f32[128]{0:T(128)S(1)}, u32[]{:S(2)}) copy-start(f32[128]{0:T(128)S(1)} %get-tuple-element.115) | copy-start | bytes 1540
  9.3 67.9 %copy-start.35 = (f32[128]{0:T(128)}, f32[128]{0:T(128)S(1)}, u32[]{:S(2)}) copy-start(f32[128]{0:T(128)S(1)} %get-tuple-element.116) | copy-start | bytes 1540
  9.3 67.9 %copy-start.36 = (f32[128]{0:T(128)}, f32[128]{0:T(128)S(1)}, u32[]{:S(2)}) copy-start(f32[128]{0:T(128)S(1)} %get-tuple-element.117) | copy-start | bytes 1540
  9.3 67.9 %copy-start.37 = (f32[128]{0:T(128)}, f32[128]{0:T(128)S(1)}, u32[]{:S(2)}) copy-start(f32[128]{0:T(128)S(1)} %get-tuple-element.118) | copy-start | bytes 1540
  16.4 175.1 %reduce-scatter.3.cloned.1.call-start = ((), (), s32[]{:S(2)}) async-start(), calls=%async_computation.3 | async-start | bytes 8912896 | tf_op jit(solution)/shard_map/reduce_scatter | solution.py:57
  88.3 198.7 %copy-start.41 = (s32[1024]{0:T(1024)S(1)}, s32[1024]{0:T(1024)}, u32[]{:S(2)}) copy-start(s32[1024]{0:T(1024)} %param.15) | copy-start | bytes 12292
  88.4 197.5 %all-reduce.101.cloned.1.call-start = ((), (), s32[]{:S(2)}) async-start(), calls=%async_computation.4 | async-start | bytes 1245184 | tf_op jit(solution)/shard_map/psum | solution.py:67
  89.2 105.0 %copy-start.43 = (f32[128]{0:T(128)}, f32[128]{0:T(128)S(1)}, u32[]{:S(2)}) copy-start(f32[128]{0:T(128)S(1)} %dynamic_slice.7) | copy-start | bytes 1540
  194.1 153.1 %all-gather.5.cloned.1.call-start = ((), (), s32[]{:S(2)}) async-start(), calls=%async_computation.5 | async-start | bytes 4456448 | tf_op jit(solution)/shard_map/all_gather | solution.py:82
  293.4 172.5 %reduce-scatter.5.cloned.1.call-start = ((), (), s32[]{:S(2)}) async-start(), calls=%async_computation.6 | async-start | bytes 8912896 | tf_op jit(solution)/shard_map/reduce_scatter | solution.py:101
  377.4 91.4 %copy-start.15 = (f32[128]{0:T(128)S(1)}, f32[128]{0:T(128)}, u32[]{:S(2)}) copy-start(f32[128]{0:T(128)} %copy-done.14) | copy-start | bytes 1540
  377.4 91.4 %copy-start.17 = (f32[128]{0:T(128)S(1)}, f32[128]{0:T(128)}, u32[]{:S(2)}) copy-start(f32[128]{0:T(128)} %copy-done.16) | copy-start | bytes 1540
  377.4 91.4 %copy-start.19 = (f32[128]{0:T(128)S(1)}, f32[128]{0:T(128)}, u32[]{:S(2)}) copy-start(f32[128]{0:T(128)} %copy-done.18) | copy-start | bytes 1540
  377.5 91.4 %copy-start.21 = (f32[128]{0:T(128)S(1)}, f32[128]{0:T(128)}, u32[]{:S(2)}) copy-start(f32[128]{0:T(128)} %copy-done.20) | copy-start | bytes 1540
  377.5 91.4 %copy-start.23 = (f32[128]{0:T(128)S(1)}, f32[128]{0:T(128)}, u32[]{:S(2)}) copy-start(f32[128]{0:T(128)} %copy-done.22) | copy-start | bytes 1540
  377.5 91.4 %copy-start.25 = (f32[128]{0:T(128)S(1)}, f32[128]{0:T(128)}, u32[]{:S(2)}) copy-start(f32[128]{0:T(128)} %copy-done.24) | copy-start | bytes 1540
  377.5 91.4 %copy-start.27 = (f32[128]{0:T(128)S(1)}, f32[128]{0:T(128)}, u32[]{:S(2)}) copy-start(f32[128]{0:T(128)} %copy-done.26) | copy-start | bytes 1540
  (27 other events, 728.7 us)
Sparse Core Ops, SparseCore 0:
  16.5 55.9 all-gather.2
  88.5 103.0 reduce-scatter.2
  195.5 90.2 all-reduce.100
  293.5 53.5 all-gather.4
  362.9 102.9 reduce-scatter.4
where the time goes:
time: 498 us
  waiting for transfers between devices  392 us (79%)
  other arithmetic  44 us (9%)
  matrix products  35 us (7%)
  between operations  16.2 us (3%)
  local copies, waits for them, and re-layouts  9.9 us (2%)
    reduce_scatter x1, waiting for transfers between devices, per_device(): lax.psum_scatter(lax.dot_general(w_cols, hidden, (((0,), (0,)), ((), ()))...  102 us
    psum x1, waiting for transfers between devices, per_device(): logits = lax.psum(part_logits, 'ch')  91.7 us
    reduce_scatter x1, waiting for transfers between devices, per_device(): lax.psum_scatter(conv_term, 'ch', scatter_dimension=0, tiled=True)  88.5 us
    all_gather x1, waiting for transfers between devices, per_device(): conv_all = lax.all_gather(conv_out, 'ch', axis=0, tiled=True)  56 us
    all_gather x1, waiting for transfers between devices, per_device(): incoming = lax.all_gather(branch_grad, 'ch', axis=0, tiled=True)  53.5 us
  transfers between devices with their start and end apart: 5, of which 5 were waited for; matrix products, arithmetic and copies ran while one was open for 3% of the time, Pallas kernels for 0%

commit v1 on v0

--- a/solution.py
+++ b/solution.py
@@ -7,6 +7,12 @@
 WIN_H = 32
 WIN_W = 32
 norm_eps = 1e-06
+
+
+def in_order(tiles, dim):
+    lengths = list(tiles.shape[1:])
+    lengths[dim] *= tiles.shape[0]
+    return jnp.moveaxis(tiles, 0, dim).reshape(lengths)
 
 
 def conv_apply(in_grid, kernel):
@@ -39,7 +45,19 @@
     inputs_wide = features.astype(jnp.float32)
     in_grid = inputs_wide.reshape(my_rows, WIN_H, WIN_W)
     conv_out = conv_apply(in_grid, dw_weight).reshape(my_rows, tok_count).astype(jnp.bfloat16)
-    conv_all = lax.all_gather(conv_out, "ch", axis=0, tiled=True)
+    size = lax.axis_size("ch")
+    pairs = [(i, (i + 1) % size) for i in range(size)]
+    back = [(b, a) for a, b in pairs]
+    lower, upper = ([], [])
+    for step in range(size - 1):
+        if step % 2 == 0:
+            lower.append(lax.ppermute(lower[-1] if lower else conv_out, "ch", pairs))
+        else:
+            upper.append(lax.ppermute(upper[-1] if upper else conv_out, "ch", back))
+    blocks = jnp.stack([*lower[::-1], conv_out, *upper])
+    shift = lax.axis_index("ch") - len(lower)
+    blocks = blocks[(jnp.arange(size) - shift) % size]
+    conv_all = in_order(blocks, 0)
     conv_wide = conv_all.astype(jnp.float32)
     tok_mean = jnp.mean(conv_wide, axis=0)
     centered = conv_wide - tok_mean[None, :]

time: 498 us -> 551 us (1.11)
  local copies, waits for them, and re-layouts: 9.9 us -> 45.5 us
  starting transfers between devices: 0.39 us -> 33.3 us
  waiting for transfers between devices: 392 us -> 371 us
    all_gather x1 -> x0, waiting for transfers between devices: 56 us -> none  [per_device(): conv_all = lax.all_gather(conv_out, 'ch', axis=0, tiled=True)]
    ppermute x0 -> x15, waiting for transfers between devices: none -> 35.2 us  [the longest x8 29.8 us: per_device(): lower.append(lax.ppermute(lower[-1] if lower else conv_out, 'ch', pairs))]
    ppermute x0 -> x15, starting transfers between devices: none -> 33.2 us  [the longest x7 32.7 us: per_device(): upper.append(lax.ppermute(upper[-1] if upper else conv_out, 'ch', back))]
    unnamed x93 -> x166, local copies, waits for them, and re-layouts: 3.12 us -> 24.9 us
    convert_element_type x0 -> x3, local copies, waits for them, and re-layouts: none -> 8.15 us  [the longest x1 7.15 us: per_device(): conv_wide = conv_all.astype(jnp.float32)]
  transfers between devices with their start and end apart: 5 -> 19, of which waited for: 5 -> 18; matrix products, arithmetic and copies ran while one was open for 3% -> 6% of each run, Pallas kernels for 0% -> 0%
where the time goes in v1:
time: 551 us; the launch traced here: 550 us
  waiting for transfers between devices  371 us (67%)
  local copies, waits for them, and re-layouts  45.5 us (8%)
  other arithmetic  45.4 us (8%)
  matrix products  37.6 us (7%)
  starting transfers between devices  33.3 us (6%)
  between operations  16.5 us (3%)
    reduce_scatter x1, waiting for transfers between devices, per_device(): lax.psum_scatter(lax.dot_general(w_cols, hidden, (((0,), (0,)), ((), ()))...  102 us
    psum x1, waiting for transfers between devices, per_device(): logits = lax.psum(part_logits, 'ch')  91.6 us
    reduce_scatter x1, waiting for transfers between devices, per_device(): lax.psum_scatter(conv_term, 'ch', scatter_dimension=0, tiled=True)  88.7 us
    all_gather x1, waiting for transfers between devices, per_device(): incoming = lax.all_gather(branch_grad, 'ch', axis=0, tiled=True)  53.7 us
    ppermute x7, starting transfers between devices, per_device(): upper.append(lax.ppermute(upper[-1] if upper else conv_out, 'ch', back))  32.7 us
    ppermute x8, waiting for transfers between devices, per_device(): lower.append(lax.ppermute(lower[-1] if lower else conv_out, 'ch', pairs))  29.8 us
    unnamed x166, local copies, waits for them, and re-layouts  24.9 us
  transfers between devices with their start and end apart: 19, of which 18 were waited for; matrix products, arithmetic and copies ran while one was open for 6% of the time, Pallas kernels for 0%

profile of v1, /device:TPU:0, one launch (start us, length us, event | category | flops | bytes accessed | tf_op | source)
XLA Modules:
  0.0 549.7 jit_solution(16679705044943498053)
XLA Ops:
  11.6 4.1 add_convert_fusion
  17.1 9.3 %collective-permute-done = bf16[128,1024]{1,0:T(8,128)(2,1)S(1)} collective-permute-done((bf16[128,1024]{1,0:T(8,128)(2,1)}, bf16[128,1024]{1,0:T(8,128)(2,1)S(1)}, u32[]{:S(2)}, u32[]{:S(2)}) %collective-permute-start) | collective-permute-done | bytes 262176 | tf_op jit(solution)/shard_map/ppermute | solution.py:54
  26.4 4.4 collective-permute-start.8
  30.8 4.1 collective-permute-done.1
  35.7 4.6 collective-permute-start.9
  44.2 4.7 collective-permute-start.10
  52.9 4.7 collective-permute-start.11
  62.2 4.7 collective-permute-start.12
  70.8 4.8 collective-permute-start.13
  79.8 4.7 collective-permute-start.14
  107.9 5.0 gather_fusion
  117.5 7.2 %copy.34 = f32[2048,1024]{0,1:T(8,128)} copy(bf16[2048,1024]{1,0:T(8,128)(2,1)} %bitcast.280) | data formatting | bytes 12582912 | tf_op jit(solution)/shard_map/convert_element_type | solution.py:61
  124.7 4.1 multiply_convert_fusion
  132.6 5.6 %convolution_bitcast_fusion = f32[2048,1024]{0,1:T(8,128)} fusion(bf16[512,2048]{1,0:T(8,128)(2,1)S(1)} %copy-done.72, f32[1024,512]{1,0:T(8,128)S(1)} %fusion.26), kind=kOutput, calls=%fused_computation.58 | convolution fusion | flops 2150105088 | bytes 12582912 | tf_op jit(solution)/shard_map/dot_general | solution.py:76
  139.0 101.9 %reduce-scatter.3.cloned.1.call-done = f32[128,1024]{0,1:T(8,128)} async-done(((f32[2048,1024]{0,1:T(8,128)}), f32[128,1024]{0,1:T(8,128)}) %reduce-scatter.3.cloned.1.call-update) | async-done | bytes 524304 | tf_op jit(solution)/shard_map/reduce_scatter | solution.py:75
  243.5 91.6 %all-reduce.101.cloned.1.call-done = f32[1024,150]{0,1:T(8,128)} async-done(((f32[1024,150]{0,1:T(8,128)}), f32[1024,150]{0,1:T(8,128)}) %all-reduce.101.cloned.1.call-update) | async-done | bytes 614416 | tf_op jit(solution)/shard_map/psum | solution.py:85
  342.8 53.7 %all-gather.2.cloned.1.call-done = bf16[2048,1024]{0,1:T(8,128)(2,1)} async-done(((bf16[128,1024]{0,1:T(8,128)(2,1)}), bf16[2048,1024]{0,1:T(8,128)(2,1)}) %all-gather.2.cloned.1.call-update) | async-done | bytes 4194320 | tf_op jit(solution)/shard_map/all_gather | solution.py:100
  396.5 6.5 %fusion.8 = bf16[512,1024]{0,1:T(8,128)(2,1)S(1)} fusion(f32[1024,512]{1,0:T(8,128)} %copy-done.8, bf16[2048,1024]{0,1:T(8,128)(2,1)} %all-gather.2.cloned.1.call-done, bf16[512,2048]{1,0:T(8,128)(2,1)} %param.13), kind=kOutput, calls=%fused_computation.66 | convolution fusion | flops 2152726528 | bytes 9437184 | tf_op jit(solution)/shard_map/dot_general | solution.py:102
  403.0 6.0 %fusion.2 = (f32[1024]{0:T(1024)S(1)}, f32[1024,2048]{1,0:T(8,128)S(1)}) fusion(f32[2048,1024]{0,1:T(8,128)} %copy.34, f32[2048]{0:T(1024)S(1)} %copy-done.27, f32[1024]{0:T(1024)S(1)} %add_rsqrt_fusion, f32[1024]{0:T(1024)S(1)} %broadcast_multiply_fusion.51, bf16[512,1024]{0,1:T(8,128)(2,1)S(1)} %fusion.8, bf16[512,2048]{1,0:T(8,128)(2,1)S(1)} %copy-done), kind=kOutput, calls=%fused_computation.5 | convolution fusion | flops 2157968384 | bytes 19943424 | tf_op jit(solution)/shard_map/dot_general | solution.py:110
  409.7 5.2 fusion.1
  417.8 7.0 %fusion.27 = f32[512,2048]{1,0:T(8,128)} fusion(bf16[512,1024]{0,1:T(8,128)(2,1)S(1)} %copy-done.7, bf16[2048,1024]{0,1:T(8,128)(2,1)} %copy-done.3), kind=kOutput, calls=%fused_computation.275 | convolution fusion | flops 2147483648 | bytes 9437184 | tf_op jit(solution)/shard_map/dot_general | solution.py:107
  424.9 4.5 fusion.23
  429.5 88.7 %reduce-scatter.5.cloned.1.call-done = f32[128,1024]{0,1:T(8,128)} async-done(((f32[2048,1024]{0,1:T(8,128)}), f32[128,1024]{0,1:T(8,128)}) %reduce-scatter.5.cloned.1.call-update) | async-done | bytes 524304 | tf_op jit(solution)/shard_map/reduce_scatter | solution.py:119
  524.7 5.8 %pad_add_fusion = f32[128,38,38]{0,2,1:T(8,128)S(1)} fusion(f32[128,32,32]{0,2,1:T(8,128)S(1)} %get-tuple-element.66, f32[128,32,32]{0,2,1:T(8,128)S(1)} %get-tuple-element.67, f32[128,32,32]{0,2,1:T(8,128)S(1)} %get-tuple-element.68, f32[128,32,32]{0,2,1:T(8,128)S(1)} %get-tuple-element.69, f32[128,32,32]{0,2,1:T(8,128)S(1)} %get-tuple-element.70, ...), kind=kLoop, calls=%fused_computation.73 | loop fusion | flops 7762944 | bytes 23283712 | tf_op jit(solution)/shard_map/transpose(jvp())/add_any | solution.py:28
  (232 shorter events, 90.2 us)
Async XLA Ops:
  7.2 121.7 %copy-start = (bf16[512,2048]{1,0:T(8,128)(2,1)S(1)}, bf16[512,2048]{1,0:T(8,128)(2,1)}, u32[]{:S(2)}) copy-start(bf16[512,2048]{1,0:T(8,128)(2,1)} %param.12) | copy-start | bytes 6291460
  7.2 233.7 %reduce-scatter.3.cloned.1.call-start = ((), (), s32[]{:S(2)}) async-start(), calls=%async_computation.2 | async-start | bytes 8912896 | tf_op jit(solution)/shard_map/reduce_scatter | solution.py:75
  16.7 9.7 %collective-permute-start = (bf16[128,1024]{1,0:T(8,128)(2,1)}, bf16[128,1024]{1,0:T(8,128)(2,1)S(1)}, u32[]{:S(2)}, u32[]{:S(2)}) collective-permute-start(bf16[128,1024]{1,0:T(8,128)(2,1)} %copy.27), channel_id=1, source_target_pairs={{0,1},{1,2},{2,3},{3,4},{4,5},{5,6},{6,7},{7,8},{8,9},{9,10},{10,1... | collective-permute-start | bytes 786440 | tf_op jit(solution)/shard_map/ppermute | solution.py:54
  26.4 8.5 %collective-permute-start.1 = (bf16[128,1024]{1,0:T(8,128)(2,1)S(1)}, bf16[128,1024]{1,0:T(8,128)(2,1)S(1)}, u32[]{:S(2)}, u32[]{:S(2)}) collective-permute-start(bf16[128,1024]{1,0:T(8,128)(2,1)S(1)} %collective-permute-done), channel_id=1, source_target_pairs={{0,1},{1,2},{2,3},{3,4},{4,5},{5,6},{6,7},{7,8},{8,9},{9,10},{10,1... | collective-permute-start | bytes 786440 | tf_op jit(solution)/shard_map/ppermute | solution.py:54
  26.4 8.6 %collective-permute-start.8 = (bf16[128,1024]{1,0:T(8,128)(2,1)}, bf16[128,1024]{1,0:T(8,128)(2,1)S(1)}, u32[]{:S(2)}, u32[]{:S(2)}) collective-permute-start(bf16[128,1024]{1,0:T(8,128)(2,1)} %copy.27), channel_id=1, source_target_pairs={{1,0},{2,1},{3,2},{4,3},{5,4},{6,5},{7,6},{8,7},{9,8},{10,9},{11,1... | collective-permute-start | bytes 786440 | tf_op jit(solution)/shard_map/ppermute | solution.py:56
  34.9 8.6 %collective-permute-start.2 = (bf16[128,1024]{1,0:T(8,128)(2,1)S(1)}, bf16[128,1024]{1,0:T(8,128)(2,1)S(1)}, u32[]{:S(2)}, u32[]{:S(2)}) collective-permute-start(bf16[128,1024]{1,0:T(8,128)(2,1)S(1)} %collective-permute-done.1), channel_id=1, source_target_pairs={{0,1},{1,2},{2,3},{3,4},{4,5},{5,6},{6,7},{7,8},{8,9},{9,10},{10,1... | collective-permute-start | bytes 786440 | tf_op jit(solution)/shard_map/ppermute | solution.py:54
  35.7 8.5 %collective-permute-start.9 = (bf16[128,1024]{1,0:T(8,128)(2,1)S(1)}, bf16[128,1024]{1,0:T(8,128)(2,1)S(1)}, u32[]{:S(2)}, u32[]{:S(2)}) collective-permute-start(bf16[128,1024]{1,0:T(8,128)(2,1)S(1)} %collective-permute-done.8), channel_id=1, source_target_pairs={{1,0},{2,1},{3,2},{4,3},{5,4},{6,5},{7,6},{8,7},{9,8},{10,9},{11,1... | collective-permute-start | bytes 786440 | tf_op jit(solution)/shard_map/ppermute | solution.py:56
  43.5 8.6 %collective-permute-start.3 = (bf16[128,1024]{1,0:T(8,128)(2,1)S(1)}, bf16[128,1024]{1,0:T(8,128)(2,1)S(1)}, u32[]{:S(2)}, u32[]{:S(2)}) collective-permute-start(bf16[128,1024]{1,0:T(8,128)(2,1)S(1)} %collective-permute-done.2), channel_id=1, source_target_pairs={{0,1},{1,2},{2,3},{3,4},{4,5},{5,6},{6,7},{7,8},{8,9},{9,10},{10,1... | collective-permute-start | bytes 786440 | tf_op jit(solution)/shard_map/ppermute | solution.py:54
  44.2 8.6 %collective-permute-start.10 = (bf16[128,1024]{1,0:T(8,128)(2,1)S(1)}, bf16[128,1024]{1,0:T(8,128)(2,1)S(1)}, u32[]{:S(2)}, u32[]{:S(2)}) collective-permute-start(bf16[128,1024]{1,0:T(8,128)(2,1)S(1)} %collective-permute-done.9), channel_id=1, source_target_pairs={{1,0},{2,1},{3,2},{4,3},{5,4},{6,5},{7,6},{8,7},{9,8},{10,9},{11,1... | collective-permute-start | bytes 786440 | tf_op jit(solution)/shard_map/ppermute | solution.py:56
  52.1 8.6 %collective-permute-start.4 = (bf16[128,1024]{1,0:T(8,128)(2,1)S(1)}, bf16[128,1024]{1,0:T(8,128)(2,1)S(1)}, u32[]{:S(2)}, u32[]{:S(2)}) collective-permute-start(bf16[128,1024]{1,0:T(8,128)(2,1)S(1)} %collective-permute-done.3), channel_id=1, source_target_pairs={{0,1},{1,2},{2,3},{3,4},{4,5},{5,6},{6,7},{7,8},{8,9},{9,10},{10,1... | collective-permute-start | bytes 786440 | tf_op jit(solution)/shard_map/ppermute | solution.py:54
  52.9 8.6 %collective-permute-start.11 = (bf16[128,1024]{1,0:T(8,128)(2,1)S(1)}, bf16[128,1024]{1,0:T(8,128)(2,1)S(1)}, u32[]{:S(2)}, u32[]{:S(2)}) collective-permute-start(bf16[128,1024]{1,0:T(8,128)(2,1)S(1)} %collective-permute-done.10), channel_id=1, source_target_pairs={{1,0},{2,1},{3,2},{4,3},{5,4},{6,5},{7,6},{8,7},{9,8},{10,9},{11,1... | collective-permute-start | bytes 786440 | tf_op jit(solution)/shard_map/ppermute | solution.py:56
  60.7 8.6 %collective-permute-start.5 = (bf16[128,1024]{1,0:T(8,128)(2,1)S(1)}, bf16[128,1024]{1,0:T(8,128)(2,1)S(1)}, u32[]{:S(2)}, u32[]{:S(2)}) collective-permute-start(bf16[128,1024]{1,0:T(8,128)(2,1)S(1)} %collective-permute-done.4), channel_id=1, source_target_pairs={{0,1},{1,2},{2,3},{3,4},{4,5},{5,6},{6,7},{7,8},{8,9},{9,10},{10,1... | collective-permute-start | bytes 786440 | tf_op jit(solution)/shard_map/ppermute | solution.py:54
  62.2 8.6 %collective-permute-start.12 = (bf16[128,1024]{1,0:T(8,128)(2,1)S(1)}, bf16[128,1024]{1,0:T(8,128)(2,1)}, u32[]{:S(2)}, u32[]{:S(2)}) collective-permute-start(bf16[128,1024]{1,0:T(8,128)(2,1)S(1)} %collective-permute-done.11), channel_id=1, source_target_pairs={{1,0},{2,1},{3,2},{4,3},{5,4},{6,5},{7,6},{8,7},{9,8},{10,9},{11,1... | collective-permute-start | bytes 786440 | tf_op jit(solution)/shard_map/ppermute | solution.py:56
  69.3 8.7 %collective-permute-start.6 = (bf16[128,1024]{1,0:T(8,128)(2,1)S(1)}, bf16[128,1024]{1,0:T(8,128)(2,1)}, u32[]{:S(2)}, u32[]{:S(2)}) collective-permute-start(bf16[128,1024]{1,0:T(8,128)(2,1)S(1)} %collective-permute-done.5), channel_id=1, source_target_pairs={{0,1},{1,2},{2,3},{3,4},{4,5},{5,6},{6,7},{7,8},{8,9},{9,10},{10,1... | collective-permute-start | bytes 786440 | tf_op jit(solution)/shard_map/ppermute | solution.py:54
  70.8 9.0 %collective-permute-start.13 = (bf16[128,1024]{1,0:T(8,128)(2,1)}, bf16[128,1024]{1,0:T(8,128)(2,1)}, u32[]{:S(2)}, u32[]{:S(2)}) collective-permute-start(bf16[128,1024]{1,0:T(8,128)(2,1)} %collective-permute-done.12), channel_id=1, source_target_pairs={{1,0},{2,1},{3,2},{4,3},{5,4},{6,5},{7,6},{8,7},{9,8},{10,9},{11,1... | collective-permute-start | bytes 786440 | tf_op jit(solution)/shard_map/ppermute | solution.py:56
  78.0 8.8 %collective-permute-start.7 = (bf16[128,1024]{1,0:T(8,128)(2,1)}, bf16[128,1024]{1,0:T(8,128)(2,1)}, u32[]{:S(2)}, u32[]{:S(2)}) collective-permute-start(bf16[128,1024]{1,0:T(8,128)(2,1)} %collective-permute-done.6), channel_id=1, source_target_pairs={{0,1},{1,2},{2,3},{3,4},{4,5},{5,6},{6,7},{7,8},{8,9},{9,10},{10,1... | collective-permute-start | bytes 786440 | tf_op jit(solution)/shard_map/ppermute | solution.py:54
  79.8 27.4 %collective-permute-start.14 = (bf16[128,1024]{1,0:T(8,128)(2,1)}, bf16[128,1024]{1,0:T(8,128)(2,1)S(1)}, u32[]{:S(2)}, u32[]{:S(2)}) collective-permute-start(bf16[128,1024]{1,0:T(8,128)(2,1)} %collective-permute-done.13), channel_id=1, source_target_pairs={{1,0},{2,1},{3,2},{4,3},{5,4},{6,5},{7,6},{8,7},{9,8},{10,9},{11,1... | collective-permute-start | bytes 786440 | tf_op jit(solution)/shard_map/ppermute | solution.py:56
  138.2 198.1 %copy-start.68 = (s32[1024]{0:T(1024)S(1)}, s32[1024]{0:T(1024)}, u32[]{:S(2)}) copy-start(s32[1024]{0:T(1024)} %param.15) | copy-start | bytes 12292
  138.2 197.0 %all-reduce.101.cloned.1.call-start = ((), (), s32[]{:S(2)}) async-start(), calls=%async_computation.3 | async-start | bytes 1245184 | tf_op jit(solution)/shard_map/psum | solution.py:85
  139.0 104.5 %copy-start.70 = (f32[128]{0:T(128)}, f32[128]{0:T(128)S(1)}, u32[]{:S(2)}) copy-start(f32[128]{0:T(128)S(1)} %dynamic_slice.7) | copy-start | bytes 1540
  243.5 153.1 %all-gather.2.cloned.1.call-start = ((), (), s32[]{:S(2)}) async-start(), calls=%async_computation.4 | async-start | bytes 4456448 | tf_op jit(solution)/shard_map/all_gather | solution.py:100
  342.8 175.4 %reduce-scatter.5.cloned.1.call-start = ((), (), s32[]{:S(2)}) async-start(), calls=%async_computation.5 | async-start | bytes 8912896 | tf_op jit(solution)/shard_map/reduce_scatter | solution.py:119
  424.8 93.4 %copy-start.43 = (f32[128]{0:T(128)S(1)}, f32[128]{0:T(128)}, u32[]{:S(2)}) copy-start(f32[128]{0:T(128)} %copy-done.42) | copy-start | bytes 1540
  424.8 93.4 %copy-start.45 = (f32[128]{0:T(128)S(1)}, f32[128]{0:T(128)}, u32[]{:S(2)}) copy-start(f32[128]{0:T(128)} %copy-done.44) | copy-start | bytes 1540
  (70 other events, 2732.3 us)
Sparse Core Ops, SparseCore 0:
  138.3 102.5 reduce-scatter.2
  244.9 90.2 all-reduce.100
  342.9 53.5 all-gather.1
  415.1 103.0 reduce-scatter.4
